TPU v7x, 32 devices: a whole 2x2x4 slice. The times are simulated.
32 devices in a mesh: groups: 2 (over x), shard: 8 (over z, y), sub: 2 (over core).
Axes of the slice: x: 2, y: 2, z: 4, core: 2. Of those that a mesh axis runs over, the one named last changes fastest.
Arguments:
- queries: bfloat16 [256, 32, 128], P(('groups', 'shard', 'sub')), parts along dimension 0, may hold values from -1.796875 to 1.796875
- passages: bfloat16 [2048, 128, 128], P(('shard', 'sub')), may hold values from -1.796875 to 1.796875
- passage_len: int32 [2048], P(('shard', 'sub')), may hold values from 16 to 128, as said below
- slot_query: int32 [32, 16, 24], P('groups', ('shard', 'sub')), parts along dimension 0, may hold values from 0 to 7
- slot_passage: int32 [32, 16, 24], P('groups', ('shard', 'sub')), parts along dimension 0, may hold values from 0 to 127
- slot_count: int32 [32, 16], P('groups', ('shard', 'sub')), parts along dimension 0, may hold values from 1 to 24, as said below
Outputs:
- slot_score: float32 [32, 16, 24], P(('groups', 'shard', 'sub')), parts along dimension 0
There are 2 independent parts, one for each index of `groups`. A program takes and returns all parts, laid end to end along the dimension named above; an argument that names none is the same for every part. Nothing has to cross between parts.
Inputs may be any that keep to these rules, and one draw needn't show every extreme that they name: `passage_len`: live tokens of a passage; some passage has all 128. Live slots from one source to one owner are its first slot_count entries; some owner receives 24 live slots from every source.
All inputs are finite; a program needn't handle non-finite values.
Results may differ from a plain program's by a relative error of at most 0.0003.
Values may be sent and summed in bfloat16 or wider, within the bound.
No kernel may reach another device: no remote copies, remote signals or barrier semaphores. Data moves between devices by JAX's collectives and lax.ppermute only.
A program may use at most 64 MiB of HBM per device.

v0:
```python
import functools

import jax
import jax.numpy as jnp
from jax import lax
from jax.experimental import pallas as pl
from jax.experimental.pallas import tpu as pltpu
from jax.sharding import PartitionSpec as P

GROUPS = 12
REST = 8
CHUNKS = 8
SHIFT = 8
QUERY, PASSAGE, LENGTH, COUNT = 0, 32, 64, 96


def distance(call, i):
    return (jnp.where(i == 1, 1, i * 2), i + 2, i * 2 + 5)[call]


def list_groups(sizes, pack, per_source, row_ref, total_ref, work_refs):
    me = lax.axis_index("shard")
    for call, (n, work_ref) in enumerate(zip(sizes, work_refs)):

        def list_source(i, total):
            live = row_ref[jnp.bitwise_xor(me, distance(call, i)), COUNT]
            for g in range(per_source):
                work_ref[total + g] = (i << SHIFT) + g
            return total + lax.shift_right_logical(live + pack - 1, pack.bit_length() - 1)

        total = 0
        if n <= 8:
            for i in range(n):
                total = list_source(i, total)
        else:
            total = lax.fori_loop(0, n, list_source, 0)
        for g in range(REST // 2 - 1):
            work_ref[total + g] = 0
        total_ref[call] = total


def pack_kernel(shards, *refs):
    query_hbm, passage_hbm, count_hbm, length_hbm, tokens_hbm, own_hbm, row_ref, theirs_ref, tokens_ref, own_ref, add_ref = refs[:11]
    mine_ref, query_ref, passage_ref, count_ref, length_ref, sems, own_sems, row_sem = refs[11:]
    copies = [
        pltpu.make_async_copy(src, dst, sems.at[i])
        for i, (src, dst) in enumerate(
            (
                (query_hbm, query_ref),
                (passage_hbm, passage_ref),
                (count_hbm, count_ref),
                (length_hbm, length_ref),
                (tokens_hbm, tokens_ref),
            )
        )
    ]
    size = own_ref.shape[0] // CHUNKS
    own_copies = [
        pltpu.make_async_copy(own_hbm.at[pl.ds(i * size, size)], own_ref.at[pl.ds(i * size, size)], own_sems.at[i])
        for i in range(CHUNKS)
    ]
    for copy in copies + own_copies:
        copy.start()
    row = lax.broadcasted_iota(jnp.int32, add_ref.shape, 0)
    col = lax.broadcasted_iota(jnp.int32, add_ref.shape, 1)
    q_bits = tokens_ref.shape[1].bit_length() - 1
    add_ref[...] = jnp.where(lax.shift_right_logical(row, q_bits) == col, 1.0, 0.0).astype(add_ref.dtype)
    for copy in copies:
        copy.wait()
    cap = query_ref.shape[1]
    lengths = length_ref[...].reshape(1, -1)
    counts = jnp.broadcast_to(count_ref[...].reshape(1, -1), (2 * shards, 2 * shards))
    row = lax.broadcasted_iota(jnp.int32, counts.shape, 0)
    col = lax.broadcasted_iota(jnp.int32, counts.shape, 1)
    counts = jnp.sum(jnp.where(row == col, counts, 0), axis=1, keepdims=True)
    blank = jnp.zeros((2 * shards, 32 - cap), jnp.int32)
    passage = jnp.concatenate([passage_ref[...], blank], axis=1)
    passage = jnp.concatenate([passage] * 4, axis=1)
    length = jnp.take_along_axis(jnp.broadcast_to(lengths, passage.shape), passage, axis=1)
    query = jnp.concatenate([jnp.concatenate([query_ref[...], blank], axis=1)] * 4, axis=1)
    lane = lax.broadcasted_iota(jnp.int32, passage.shape, 1)
    packed = jnp.where(lane < PASSAGE, query, jnp.where(lane < LENGTH, passage, jnp.where(lane < COUNT, length, counts)))
    packed = packed.reshape(shards, 2, 128)
    first = lax.axis_index("sub") == 0
    mine_ref[...] = jnp.where(first, packed[:, 0], packed[:, 1])
    theirs_ref[...] = jnp.where(first, packed[:, 1], packed[:, 0])
    row_copy = pltpu.make_async_copy(mine_ref, row_ref, row_sem)
    row_copy.start()
    for copy in own_copies:
        copy.wait()
    row_copy.wait()


def score_kernel(shards, calls, call, pack, cap, *refs):
    distances = calls[call]
    n = len(distances)
    p = 1 if call == 1 else n
    if call == 0:
        (own_rows, rows), refs = refs[:2], refs[2:]
        refs, (out_ref, *outs, query_ref, best_ref, row_sem) = refs[: p + 3], refs[p + 3 :]
        made = (own_rows, *outs[: len(calls) + 1]), outs[len(calls) + 1 :]
        lists = [(row_ref, total_ref, work_ref) for row_ref, total_ref, work_ref, *_ in made]
        copy = pltpu.make_async_copy(rows, made[1][0], row_sem)
        copy.start()
    else:
        lists = [refs[:3], refs[3:6]]
        refs, (out_ref, query_ref, best_ref) = refs[6:-3], refs[-3:]
    pieces, passage_refs, add_ref, earlier = refs[:p], refs[p : p + 2], refs[p + 2], refs[p + 3 :]
    q_tok, width = query_ref.shape[2:]
    tok_slots = passage_refs[0].shape[1]
    per_source = best_ref.shape[0]
    lanes = pack * q_tok
    q_bits = q_tok.bit_length() - 1
    me, core = lax.axis_index("shard"), lax.axis_index("sub")
    if call == 1:
        query_ref[...] = pieces[0][...]
    else:
        for i, piece in enumerate(reversed(pieces)):
            query_ref[i] = piece[...]
    best_ref[...] = jnp.zeros_like(best_ref)
    token = lax.broadcasted_iota(jnp.int32, (tok_slots, lanes), 0)
    place = lax.shift_right_logical(lax.broadcasted_iota(jnp.int32, (1, lanes), 1), q_bits)
    blank = jnp.zeros((q_tok, width), query_ref.dtype)

    for which, passages in enumerate(passage_refs):
        meta_ref, total_ref, work_ref = lists[which]
        owner = core if which == 0 else 1 - core
        if call == 0:
            if which == 1:
                copy.wait()
            list_groups(tuple(map(len, calls)), pack, per_source, *made[which][:2], made[which][2:])
        total = total_ref[call]

        def one_step(first_group, groups):
            for j in range(groups):
                work = work_ref[first_group + j]
                i, g = lax.shift_right_logical(work, SHIFT), jnp.bitwise_and(work, (1 << SHIFT) - 1)
                shard = jnp.bitwise_xor(me, distance(call, i))
                rows, cols, limit = [], [], jnp.zeros((1, lanes), jnp.int32)
                for a in range(pack):
                    slot = g * pack + a
                    query, passage = meta_ref[shard, QUERY + slot], meta_ref[shard, PASSAGE + slot]
                    rows.append(jnp.concatenate([blank] * a + [query_ref[i, query]] + [blank] * (pack - 1 - a), axis=1))
                    cols.append(passages[passage])
                    limit = jnp.where(place == a, meta_ref[shard, LENGTH + slot], limit)
                sims = lax.dot_general(
                    jnp.concatenate(cols, axis=1), jnp.concatenate(rows, axis=0),
                    (((1,), (1,)), ((), ())), preferred_element_type=jnp.float32,
                )
                best = jnp.max(jnp.where(token < limit, sims, -1e30), axis=0, keepdims=True)
                best = jnp.where(place + g * pack < meta_ref[shard, COUNT], best, 0.0)
                best_ref[g, pl.ds(i * 2 + owner, 1), :] = best

        steps = lax.div(total + GROUPS - REST - 1, GROUPS)
        rest = total - steps * GROUPS

        @pl.loop(0, steps)
        def _(step):
            one_step(step * GROUPS, GROUPS)

        @pl.when(rest > REST // 2)
        def _():
            one_step(steps * GROUPS, REST)

        @pl.when((rest > 0) & (rest <= REST // 2))
        def _():
            one_step(steps * GROUPS, REST // 2)

    best = jnp.concatenate([best_ref[g] for g in range(per_source)], axis=1)
    high = best.astype(jnp.bfloat16)
    rest = best - high.astype(jnp.float32)
    middle = rest.astype(jnp.bfloat16)
    low = (rest - middle.astype(jnp.float32)).astype(jnp.bfloat16)
    parts = jnp.dot(jnp.concatenate([high, middle, low], axis=0), add_ref[...], preferred_element_type=jnp.float32)
    rows = best.shape[0]
    score = (parts[:rows] + parts[rows : 2 * rows] + parts[2 * rows :]) * (1.0 / q_tok)
    if call < 2:
        out_ref[...] = score[:, :cap]
        return
    for scores, at in zip((*(ref[...] for ref in earlier), score[:, :cap]), ((0, 1, *range(4, shards, 2)), (2, 3), distances)):
        for i, d in enumerate(at):
            out_ref[pl.ds((shards - 1 - jnp.bitwise_xor(me, d)) * 2, 2), :] = scores[2 * i : 2 * i + 2]


def pair_kernel(one_ref, other_ref, out_ref):
    out_ref[0] = one_ref[...]
    out_ref[1] = other_ref[...]


def order_kernel(back_ref, out_ref):
    shards = back_ref.shape[0] // 2
    for i in range(shards):
        out_ref[0, 2 * i : 2 * i + 2] = back_ref[2 * (shards - 1 - i) : 2 * (shards - i)]


def on_device(shards, queries, passages, passage_len, slot_query, slot_passage, slot_count):
    sources, _, cap = slot_query.shape
    q_dev, q_tok, width = queries.shape
    pack = 128 // q_tok
    per_source = -(-cap // pack)
    swap = [(0, 1), (1, 0)]
    vmem, hbm, smem, anywhere = (pl.BlockSpec(memory_space=space) for space in (pltpu.VMEM, pltpu.HBM, pltpu.SMEM, pl.ANY))
    params = pltpu.CompilerParams(vmem_limit_bytes=12 * 1024 * 1024)
    row = jax.ShapeDtypeStruct((shards, 128), jnp.int32)

    def placed(space, *arrays):
        return [pltpu.with_memory_space_constraint(x, space) for x in arrays]

    def swapped(piece, d):
        return lax.ppermute(piece, "shard", [(i, i ^ d) for i in range(shards)])

    pieces = [queries, swapped(queries, 1)] + [None] * (shards - 2)
    for d in range(4, shards, 2):
        pieces[d] = swapped(queries, d)
    other_passages = lax.ppermute(passages, "sub", swap)

    calls = ((0, 1, *range(4, shards, 2)), (2, 3), range(5, shards, 2))
    sizes = tuple(map(len, calls))
    listed = [
        pltpu.SMEM(row.shape, row.dtype),
        pltpu.SMEM((len(calls),), jnp.int32),
        *(pltpu.SMEM((n * per_source + 2 * GROUPS,), jnp.int32) for n in sizes),
    ]
    mine, theirs, own_queries, own_passages, add = pl.pallas_call(
        functools.partial(pack_kernel, shards),
        out_shape=[
            pltpu.SMEM(row.shape, row.dtype), row, *(jax.ShapeDtypeStruct(x.shape, x.dtype) for x in (queries, passages)),
            jax.ShapeDtypeStruct((per_source * 128, 128), jnp.bfloat16),
        ],
        in_specs=[hbm] * 6,
        out_specs=[smem] + [vmem] * 4,
        scratch_shapes=[
            pltpu.VMEM(row.shape, row.dtype),
            pltpu.VMEM((sources, cap), jnp.int32),
            pltpu.VMEM((sources, cap), jnp.int32),
            pltpu.VMEM((sources,), jnp.int32),
            pltpu.VMEM(passage_len.shape, jnp.int32),
            pltpu.SemaphoreType.DMA((5,)),
            pltpu.SemaphoreType.DMA((CHUNKS,)),
            pltpu.SemaphoreType.DMA,
        ],
        compiler_params=params,
    )(*placed(pltpu.HBM, slot_query.reshape(sources, cap), slot_passage.reshape(sources, cap), slot_count.reshape(sources), passage_len, queries, passages))
    both = pl.pallas_call(
        pair_kernel,
        out_shape=jax.ShapeDtypeStruct((2, *queries.shape), queries.dtype),
        in_specs=[vmem] * 2,
        out_specs=vmem,
        compiler_params=params,
    )(own_queries, pieces[1])
    both = swapped(both, 2)
    for d in range(5, shards, 2):
        pieces[d] = swapped(pieces[1], d - 1) if d == shards - 1 else swapped(pieces[d - 1], 1)
    theirs, _ = lax.optimization_barrier((theirs, other_passages))
    other = lax.ppermute(theirs, "sub", swap)

    def scored(parts, lists, *earlier):
        call = len(earlier)
        n = sizes[call]
        scores = jax.ShapeDtypeStruct((2 * n if call < 2 else sources, cap), jnp.float32)
        if call:
            given = [x for rows, totals, *works in lists for x in placed(pltpu.SMEM, rows, totals, works[call])]
        else:
            given = [*placed(pltpu.SMEM, lists[0]), lists[1]]
        return pl.pallas_call(
            functools.partial(score_kernel, shards, calls, call, pack, cap),
            out_shape=scores if call else [scores, *listed[1:], *listed],
            in_specs=([smem] * 6 if call else [smem, anywhere]) + [vmem] * (len(parts) + 3 + call),
            out_specs=vmem if call else [vmem] + [smem] * (2 * len(listed) - 1),
            scratch_shapes=[
                pltpu.VMEM((n, *queries.shape), queries.dtype),
                pltpu.VMEM((per_source, 2 * n, 128), jnp.float32),
                *([] if call else [pltpu.SemaphoreType.DMA]),
            ],
            compiler_params=params,
            cost_estimate=pl.CostEstimate(flops=1_000_000_000, bytes_accessed=9_000_000, transcendentals=0),
        )(*given, *parts, *placed(pltpu.VMEM, own_passages, other_passages), add, *earlier)

    pieces[0] = own_queries
    near, _, far = calls
    first_scores, *made = scored([pieces[d] for d in reversed(near)], [mine, other])
    lists = [mine, *made[: len(calls) + 1]], made[len(calls) + 1 :]
    next_scores = scored([both], lists, first_scores)
    scores = scored([pieces[d] for d in reversed(far)], lists, first_scores, next_scores)
    order = [list(reversed(range(shards)))]
    returned = lax.all_to_all(scores, "shard", split_axis=0, concat_axis=0, axis_index_groups=order, tiled=True)
    return pl.pallas_call(
        order_kernel,
        out_shape=jax.ShapeDtypeStruct((1, sources, cap), jnp.float32),
        in_specs=[vmem],
        out_specs=vmem,
        compiler_params=params,
    )(returned)


def solution(mesh):
    return jax.shard_map(
        functools.partial(on_device, mesh.shape["shard"]),
        mesh=mesh,
        in_specs=(
            P(("groups", "shard", "sub"), None, None),
            P(("shard", "sub"), None, None),
            P(("shard", "sub")),
            P("groups", ("shard", "sub"), None),
            P("groups", ("shard", "sub"), None),
            P("groups", ("shard", "sub")),
        ),
        out_specs=P(("groups", "shard", "sub"), None, None),
        check_vma=False,
    )
```

profile of v0, /device:TPU:0, one launch (start us, length us, event | category | flops | bytes accessed | tf_op | source)
XLA Modules:
  0.0 27.1 jit_solution(396423909392836894)
XLA Ops:
  0.0 0.5 %collective-permute-start = (bf16[128,128,128]{2,1,0:T(8,128)(2,1)}, bf16[128,128,128]{2,1,0:T(8,128)(2,1)S(1)}, u32[]{:S(2)}, u32[]{:S(2)}) collective-permute-start(bf16[128,128,128]{2,1,0:T(8,128)(2,1)} %refs_5_.1), channel_id=1, source_target_pairs={{0,1},{1,0},{2,3},{3,2},{4,5},{5,4},{6,7},{7,6},{8,9},{9,8},{10,11... | collective-permute-start | bytes 12582920 | tf_op jit(solution)/shard_map/ppermute | solution.py:215
  0.5 2.5 %collective-permute-start.4 = (bf16[8,32,128]{2,1,0:T(8,128)(2,1)}, bf16[8,32,128]{2,1,0:T(8,128)(2,1)S(1)}, u32[]{:S(2)}, u32[]{:S(2)}) collective-permute-start(bf16[8,32,128]{2,1,0:T(8,128)(2,1)} %refs_4_.1), channel_id=1, source_target_pairs={{0,2},{2,0},{4,6},{6,4},{8,10},{10,8},{12,14},{14,12},{1,3},{3,1},... | collective-permute-start | bytes 196616 | tf_op jit(solution)/shard_map/ppermute | solution.py:210
  3.0 2.6 %collective-permute-start.3 = (bf16[8,32,128]{2,1,0:T(8,128)(2,1)}, bf16[8,32,128]{2,1,0:T(8,128)(2,1)S(1)}, u32[]{:S(2)}, u32[]{:S(2)}) collective-permute-start(bf16[8,32,128]{2,1,0:T(8,128)(2,1)} %refs_4_.1), channel_id=1, source_target_pairs={{0,8},{2,10},{4,12},{6,14},{8,0},{10,2},{12,4},{14,6},{1,9},{3,11}... | collective-permute-start | bytes 196616 | tf_op jit(solution)/shard_map/ppermute | solution.py:210
  5.6 1.3 %collective-permute-start.2 = (bf16[8,32,128]{2,1,0:T(8,128)(2,1)}, bf16[8,32,128]{2,1,0:T(8,128)(2,1)S(1)}, u32[]{:S(2)}, u32[]{:S(2)}) collective-permute-start(bf16[8,32,128]{2,1,0:T(8,128)(2,1)} %refs_4_.1), channel_id=1, source_target_pairs={{0,12},{2,14},{4,8},{6,10},{8,4},{10,6},{12,0},{14,2},{1,13},{3,15... | collective-permute-start | bytes 196616 | tf_op jit(solution)/shard_map/ppermute | solution.py:210
  6.9 2.9 %shard_map.64 = (s32[8,128]{1,0:T(8,128)S(4)}, s32[8,128]{1,0:T(8,128)S(1)}, bf16[8,32,128]{2,1,0:T(8,128)(2,1)S(1)}, bf16[128,128,128]{2,1,0:T(8,128)(2,1)S(1)}, bf16[768,128]{1,0:T(8,128)(2,1)S(1)}) custom-call(s32[16,24]{1,0:T(8,128)} %bitcast.7, s32[16,24]{1,0:T(8,128)} %bitcast.8, s32[16]{0:T(128)} %bitcast.9, s32[128]{0:T(128)} %refs_3_.1, ...), custom_call_target="tpu_custom_call" | custom-call | tf_op jit(solution)/shard_map/pallas_call | solution.py:224
  9.8 0.0 collective-permute-done.4.refs_4_.other_ref
  9.8 0.3 %collective-permute-start.7 = (bf16[2,8,32,128]{3,2,1,0:T(8,128)(2,1)S(1)}, bf16[2,8,32,128]{3,2,1,0:T(8,128)(2,1)S(1)}, u32[]{:S(2)}, u32[]{:S(2)}) collective-permute-start(bf16[2,8,32,128]{3,2,1,0:T(8,128)(2,1)S(1)} %shard_map.66), channel_id=1, source_target_pairs={{0,4},{2,6},{4,0},{6,2},{8,12},{10,14},{12,8},{14,10},{1,5},{3,7},... | collective-permute-start | bytes 393224 | tf_op jit(solution)/shard_map/ppermute | solution.py:210
  10.1 0.0 collective-permute-done.refs_7_.refs_8_.refs_9_
  10.1 0.0 collective-permute-start.1
  10.1 2.9 %collective-permute-start.5 = (bf16[8,32,128]{2,1,0:T(8,128)(2,1)S(1)}, bf16[8,32,128]{2,1,0:T(8,128)(2,1)S(1)}, u32[]{:S(2)}, u32[]{:S(2)}) collective-permute-start(bf16[8,32,128]{2,1,0:T(8,128)(2,1)S(1)} %collective-permute-done.4.refs_4_.other_ref), channel_id=1, source_target_pairs={{0,12},{2,14},{4,8},{6,10},{8,4},{10,6},{12,0},{14,2},{1,13},{3,15... | collective-permute-start | bytes 196616 | tf_op jit(solution)/shard_map/ppermute | solution.py:210
  13.1 0.0 collective-permute-done.3.refs_3_
  13.1 1.0 %collective-permute-start.6 = (bf16[8,32,128]{2,1,0:T(8,128)(2,1)S(1)}, bf16[8,32,128]{2,1,0:T(8,128)(2,1)S(1)}, u32[]{:S(2)}, u32[]{:S(2)}) collective-permute-start(bf16[8,32,128]{2,1,0:T(8,128)(2,1)S(1)} %collective-permute-done.3.refs_3_), channel_id=1, source_target_pairs={{0,2},{2,0},{4,6},{6,4},{8,10},{10,8},{12,14},{14,12},{1,3},{3,1},... | collective-permute-start | bytes 196616 | tf_op jit(solution)/shard_map/ppermute | solution.py:210
  14.1 0.0 collective-permute-done.2.refs_2_
  14.1 0.0 collective-permute-done.1.refs_1_
  14.1 1.5 %shard_map.65 = (f32[8,24]{1,0:T(8,128)S(1)}, s32[3]{0:T(128)S(4)}, s32[48]{0:T(128)S(4)}, s32[36]{0:T(128)S(4)}, s32[36]{0:T(128)S(4)}, /*index=5*/s32[8,128]{1...) custom-call(s32[8,128]{1,0:T(8,128)S(4)} %get-tuple-element.19.refs_0_, ...), custom_call_target="tpu_custom_call" | custom-call | flops 1000000000 | bytes 9000000 | tf_op jit(solution)/shard_map/pallas_call | solution.py:265
  15.6 0.0 collective-permute-done.7.refs_6_
  15.6 0.8 %shard_map.67.refs_12_ = f32[4,24]{1,0:T(4,128)S(1)} custom-call(s32[8,128]{1,0:T(8,128)S(4)} %get-tuple-element.19.refs_0_, s32[3]{0:T(128)S(4)} %get-tuple-element.25.refs_1_, s32[36]{0:T(128)S(4)} %get-tuple-element.31.refs_2_, s32[8,128]{1,0:T(8,128)S(4)} %get-tuple-element.27.refs_3_, s32[3]{0:T(128)S(4)} %get-tuple-element.28.refs_4_, ...), custom_call_target="tpu_custom_call" | custom-call | flops 1000000000 | bytes 9000000 | tf_op jit(solution)/shard_map/pallas_call | solution.py:265
  16.4 1.1 %collective-permute-done.5.refs_6_ = bf16[8,32,128]{2,1,0:T(8,128)(2,1)S(1)} collective-permute-done((bf16[8,32,128]{2,1,0:T(8,128)(2,1)S(1)}, bf16[8,32,128]{2,1,0:T(8,128)(2,1)S(1)}, u32[]{:S(2)}, u32[]{:S(2)}) %collective-permute-start.5) | collective-permute-done | bytes 65568 | tf_op jit(solution)/shard_map/ppermute | solution.py:210
  17.5 0.0 collective-permute-done.6.refs_7_
  17.5 0.8 %shard_map.68 = f32[16,24]{1,0:T(8,128)S(1)} custom-call(s32[8,128]{1,0:T(8,128)S(4)} %get-tuple-element.19.refs_0_, s32[3]{0:T(128)S(4)} %get-tuple-element.25.refs_1_, s32[36]{0:T(128)S(4)} %get-tuple-element.26.refs_2_, s32[8,128]{1,0:T(8,128)S(4)} %get-tuple-element.27.refs_3_, s32[3]{0:T(128)S(4)} %get-tuple-element.28.refs_4_, ...), custom_call_target="tpu_custom_call" | custom-call | flops 1000000000 | bytes 9000000 | tf_op jit(solution)/shard_map/pallas_call | solution.py:265
  18.3 8.2 %all_to_all.11 = f32[8,2,24]{2,1,0:T(2,128)S(1)} all-to-all(f32[8,2,24]{2,1,0:T(2,128)S(1)} %bitcast.5), channel_id=1, replica_groups={{14,12,10,8,6,4,2,0},{15,13,11,9,7,5,3,1},{30,28,26,24,22,20,18,16},{31..., dimensions={0} | all-to-all | bytes 3072 | tf_op jit(solution)/shard_map/all_to_all | solution.py:286
  26.5 0.6 %shard_map.69 = f32[1,16,24]{2,1,0:T(8,128)} custom-call(f32[16,24]{1,0:T(8,128)S(1)} %bitcast.6), custom_call_target="tpu_custom_call" | custom-call | tf_op jit(solution)/shard_map/pallas_call | solution.py:287
  (1 shorter events, 0.0 us)
Async XLA Ops:
  0.0 10.1 %collective-permute-start = (bf16[128,128,128]{2,1,0:T(8,128)(2,1)}, bf16[128,128,128]{2,1,0:T(8,128)(2,1)S(1)}, u32[]{:S(2)}, u32[]{:S(2)}) collective-permute-start(bf16[128,128,128]{2,1,0:T(8,128)(2,1)} %refs_5_.1), channel_id=1, source_target_pairs={{0,1},{1,0},{2,3},{3,2},{4,5},{5,4},{6,7},{7,6},{8,9},{9,8},{10,11... | collective-permute-start | bytes 12582920 | tf_op jit(solution)/shard_map/ppermute | solution.py:215
  0.5 9.3 %collective-permute-start.4 = (bf16[8,32,128]{2,1,0:T(8,128)(2,1)}, bf16[8,32,128]{2,1,0:T(8,128)(2,1)S(1)}, u32[]{:S(2)}, u32[]{:S(2)}) collective-permute-start(bf16[8,32,128]{2,1,0:T(8,128)(2,1)} %refs_4_.1), channel_id=1, source_target_pairs={{0,2},{2,0},{4,6},{6,4},{8,10},{10,8},{12,14},{14,12},{1,3},{3,1},... | collective-permute-start | bytes 196616 | tf_op jit(solution)/shard_map/ppermute | solution.py:210
  3.0 10.1 %collective-permute-start.3 = (bf16[8,32,128]{2,1,0:T(8,128)(2,1)}, bf16[8,32,128]{2,1,0:T(8,128)(2,1)S(1)}, u32[]{:S(2)}, u32[]{:S(2)}) collective-permute-start(bf16[8,32,128]{2,1,0:T(8,128)(2,1)} %refs_4_.1), channel_id=1, source_target_pairs={{0,8},{2,10},{4,12},{6,14},{8,0},{10,2},{12,4},{14,6},{1,9},{3,11}... | collective-permute-start | bytes 196616 | tf_op jit(solution)/shard_map/ppermute | solution.py:210
  5.6 8.5 %collective-permute-start.2 = (bf16[8,32,128]{2,1,0:T(8,128)(2,1)}, bf16[8,32,128]{2,1,0:T(8,128)(2,1)S(1)}, u32[]{:S(2)}, u32[]{:S(2)}) collective-permute-start(bf16[8,32,128]{2,1,0:T(8,128)(2,1)} %refs_4_.1), channel_id=1, source_target_pairs={{0,12},{2,14},{4,8},{6,10},{8,4},{10,6},{12,0},{14,2},{1,13},{3,15... | collective-permute-start | bytes 196616 | tf_op jit(solution)/shard_map/ppermute | solution.py:210
  9.8 5.7 %collective-permute-start.7 = (bf16[2,8,32,128]{3,2,1,0:T(8,128)(2,1)S(1)}, bf16[2,8,32,128]{3,2,1,0:T(8,128)(2,1)S(1)}, u32[]{:S(2)}, u32[]{:S(2)}) collective-permute-start(bf16[2,8,32,128]{3,2,1,0:T(8,128)(2,1)S(1)} %shard_map.66), channel_id=1, source_target_pairs={{0,4},{2,6},{4,0},{6,2},{8,12},{10,14},{12,8},{14,10},{1,5},{3,7},... | collective-permute-start | bytes 393224 | tf_op jit(solution)/shard_map/ppermute | solution.py:210
  10.1 4.0 %collective-permute-start.1 = (s32[8,128]{1,0:T(8,128)S(1)}, s32[8,128]{1,0:T(8,128)S(1)}, u32[]{:S(2)}, u32[]{:S(2)}) collective-permute-start(s32[8,128]{1,0:T(8,128)S(1)} %get-tuple-element.21), channel_id=1, source_target_pairs={{0,1},{1,0},{2,3},{3,2},{4,5},{5,4},{6,7},{7,6},{8,9},{9,8},{10,11... | collective-permute-start | bytes 12296 | tf_op jit(solution)/shard_map/ppermute | solution.py:255
  10.1 7.4 %collective-permute-start.5 = (bf16[8,32,128]{2,1,0:T(8,128)(2,1)S(1)}, bf16[8,32,128]{2,1,0:T(8,128)(2,1)S(1)}, u32[]{:S(2)}, u32[]{:S(2)}) collective-permute-start(bf16[8,32,128]{2,1,0:T(8,128)(2,1)S(1)} %collective-permute-done.4.refs_4_.other_ref), channel_id=1, source_target_pairs={{0,12},{2,14},{4,8},{6,10},{8,4},{10,6},{12,0},{14,2},{1,13},{3,15... | collective-permute-start | bytes 196616 | tf_op jit(solution)/shard_map/ppermute | solution.py:210
  13.1 4.4 %collective-permute-start.6 = (bf16[8,32,128]{2,1,0:T(8,128)(2,1)S(1)}, bf16[8,32,128]{2,1,0:T(8,128)(2,1)S(1)}, u32[]{:S(2)}, u32[]{:S(2)}) collective-permute-start(bf16[8,32,128]{2,1,0:T(8,128)(2,1)S(1)} %collective-permute-done.3.refs_3_), channel_id=1, source_target_pairs={{0,2},{2,0},{4,6},{6,4},{8,10},{10,8},{12,14},{14,12},{1,3},{3,1},... | collective-permute-start | bytes 196616 | tf_op jit(solution)/shard_map/ppermute | solution.py:210
where the time goes:
time: 27.3 us; the launch traced here: 27.1 us
  starting transfers between devices  11.2 us (41%)
  blocking collectives  8.18 us (30%)
  Pallas kernels  6.6 us (24%)
  waiting for transfers between devices  1.11 us (4%)
    ppermute x6, starting transfers between devices, swapped(): return lax.ppermute(piece, 'shard', [(i, i ^ d) for i in range(shards)])  10.7 us
    all_to_all x1, blocking collectives, on_device(): lax.all_to_all(scores, 'shard', split_axis=0, concat_axis=0, axis_index_g...  8.18 us
    pallas_call x3, Pallas kernels, scored(): pl.pallas_call(functools.partial(score_kernel, shards, calls, call, pack,...  3.11 us
    pallas_call x1, Pallas kernels, on_device(): pl.pallas_call(functools.partial(pack_kernel, shards), out_shape=[pltpu.S...  2.88 us
    ppermute x6, waiting for transfers between devices, swapped(): return lax.ppermute(piece, 'shard', [(i, i ^ d) for i in range(shards)])  1.11 us
    pallas_call x1, Pallas kernels, on_device(): pl.pallas_call(order_kernel, out_shape=jax.ShapeDtypeStruct((1, sources,...  0.6 us
  transfers between devices with their start and end apart: 8, of which 1 were waited for; matrix products, arithmetic and copies ran while one was open for 0% of the time, Pallas kernels for 19%

commit v1 on v0

--- a/solution.py
+++ b/solution.py
@@ -85,7 +85,7 @@
     mine_ref[...] = jnp.where(first, packed[:, 0], packed[:, 1])
     theirs_ref[...] = jnp.where(first, packed[:, 1], packed[:, 0])
     row_copy = pltpu.make_async_copy(mine_ref, row_ref, row_sem)
-    row_copy.start()
+    row_copy.start(priority=1)
     for copy in own_copies:
         copy.wait()
     row_copy.wait()

time: 27.3 us -> 27.4 us (level)
  no operation moved by 1% of the time
where the time goes in v1:
time: 27.4 us; the launch traced here: 27.1 us
  starting transfers between devices  11.2 us (41%)
  blocking collectives  8.18 us (30%)
  Pallas kernels  6.55 us (24%)
  waiting for transfers between devices  1.16 us (4%)
    ppermute x6, starting transfers between devices, swapped(): return lax.ppermute(piece, 'shard', [(i, i ^ d) for i in range(shards)])  10.7 us
    all_to_all x1, blocking collectives, on_device(): lax.all_to_all(scores, 'shard', split_axis=0, concat_axis=0, axis_index_g...  8.18 us
    pallas_call x3, Pallas kernels, scored(): pl.pallas_call(functools.partial(score_kernel, shards, calls, call, pack,...  3.06 us
    pallas_call x1, Pallas kernels, on_device(): pl.pallas_call(functools.partial(pack_kernel, shards), out_shape=[pltpu.S...  2.88 us
    ppermute x6, waiting for transfers between devices, swapped(): return lax.ppermute(piece, 'shard', [(i, i ^ d) for i in range(shards)])  1.16 us
    pallas_call x1, Pallas kernels, on_device(): pl.pallas_call(order_kernel, out_shape=jax.ShapeDtypeStruct((1, sources,...  0.6 us
  transfers between devices with their start and end apart: 8, of which 1 were waited for; matrix products, arithmetic and copies ran while one was open for 0% of the time, Pallas kernels for 19%

profile of v1, /device:TPU:0, one launch (start us, length us, event | category | flops | bytes accessed | tf_op | source)
XLA Modules:
  0.0 27.1 jit_solution(396423909392836894)
XLA Ops:
  0.0 0.5 %collective-permute-start = (bf16[128,128,128]{2,1,0:T(8,128)(2,1)}, bf16[128,128,128]{2,1,0:T(8,128)(2,1)S(1)}, u32[]{:S(2)}, u32[]{:S(2)}) collective-permute-start(bf16[128,128,128]{2,1,0:T(8,128)(2,1)} %refs_5_.1), channel_id=1, source_target_pairs={{0,1},{1,0},{2,3},{3,2},{4,5},{5,4},{6,7},{7,6},{8,9},{9,8},{10,11... | collective-permute-start | bytes 12582920 | tf_op jit(solution)/shard_map/ppermute | solution.py:215
  0.5 2.5 %collective-permute-start.4 = (bf16[8,32,128]{2,1,0:T(8,128)(2,1)}, bf16[8,32,128]{2,1,0:T(8,128)(2,1)S(1)}, u32[]{:S(2)}, u32[]{:S(2)}) collective-permute-start(bf16[8,32,128]{2,1,0:T(8,128)(2,1)} %refs_4_.1), channel_id=1, source_target_pairs={{0,2},{2,0},{4,6},{6,4},{8,10},{10,8},{12,14},{14,12},{1,3},{3,1},... | collective-permute-start | bytes 196616 | tf_op jit(solution)/shard_map/ppermute | solution.py:210
  3.0 2.6 %collective-permute-start.3 = (bf16[8,32,128]{2,1,0:T(8,128)(2,1)}, bf16[8,32,128]{2,1,0:T(8,128)(2,1)S(1)}, u32[]{:S(2)}, u32[]{:S(2)}) collective-permute-start(bf16[8,32,128]{2,1,0:T(8,128)(2,1)} %refs_4_.1), channel_id=1, source_target_pairs={{0,8},{2,10},{4,12},{6,14},{8,0},{10,2},{12,4},{14,6},{1,9},{3,11}... | collective-permute-start | bytes 196616 | tf_op jit(solution)/shard_map/ppermute | solution.py:210
  5.6 1.3 %collective-permute-start.2 = (bf16[8,32,128]{2,1,0:T(8,128)(2,1)}, bf16[8,32,128]{2,1,0:T(8,128)(2,1)S(1)}, u32[]{:S(2)}, u32[]{:S(2)}) collective-permute-start(bf16[8,32,128]{2,1,0:T(8,128)(2,1)} %refs_4_.1), channel_id=1, source_target_pairs={{0,12},{2,14},{4,8},{6,10},{8,4},{10,6},{12,0},{14,2},{1,13},{3,15... | collective-permute-start | bytes 196616 | tf_op jit(solution)/shard_map/ppermute | solution.py:210
  6.9 2.9 %shard_map.64 = (s32[8,128]{1,0:T(8,128)S(4)}, s32[8,128]{1,0:T(8,128)S(1)}, bf16[8,32,128]{2,1,0:T(8,128)(2,1)S(1)}, bf16[128,128,128]{2,1,0:T(8,128)(2,1)S(1)}, bf16[768,128]{1,0:T(8,128)(2,1)S(1)}) custom-call(s32[16,24]{1,0:T(8,128)} %bitcast.7, s32[16,24]{1,0:T(8,128)} %bitcast.8, s32[16]{0:T(128)} %bitcast.9, s32[128]{0:T(128)} %refs_3_.1, ...), custom_call_target="tpu_custom_call" | custom-call | tf_op jit(solution)/shard_map/pallas_call | solution.py:224
  9.8 0.0 collective-permute-done.4.refs_4_.other_ref
  9.8 0.3 %collective-permute-start.7 = (bf16[2,8,32,128]{3,2,1,0:T(8,128)(2,1)S(1)}, bf16[2,8,32,128]{3,2,1,0:T(8,128)(2,1)S(1)}, u32[]{:S(2)}, u32[]{:S(2)}) collective-permute-start(bf16[2,8,32,128]{3,2,1,0:T(8,128)(2,1)S(1)} %shard_map.66), channel_id=1, source_target_pairs={{0,4},{2,6},{4,0},{6,2},{8,12},{10,14},{12,8},{14,10},{1,5},{3,7},... | collective-permute-start | bytes 393224 | tf_op jit(solution)/shard_map/ppermute | solution.py:210
  10.1 0.0 collective-permute-done.refs_7_.refs_8_.refs_9_
  10.1 0.0 collective-permute-start.1
  10.1 2.9 %collective-permute-start.5 = (bf16[8,32,128]{2,1,0:T(8,128)(2,1)S(1)}, bf16[8,32,128]{2,1,0:T(8,128)(2,1)S(1)}, u32[]{:S(2)}, u32[]{:S(2)}) collective-permute-start(bf16[8,32,128]{2,1,0:T(8,128)(2,1)S(1)} %collective-permute-done.4.refs_4_.other_ref), channel_id=1, source_target_pairs={{0,12},{2,14},{4,8},{6,10},{8,4},{10,6},{12,0},{14,2},{1,13},{3,15... | collective-permute-start | bytes 196616 | tf_op jit(solution)/shard_map/ppermute | solution.py:210
  13.1 0.0 collective-permute-done.3.refs_3_
  13.1 1.0 %collective-permute-start.6 = (bf16[8,32,128]{2,1,0:T(8,128)(2,1)S(1)}, bf16[8,32,128]{2,1,0:T(8,128)(2,1)S(1)}, u32[]{:S(2)}, u32[]{:S(2)}) collective-permute-start(bf16[8,32,128]{2,1,0:T(8,128)(2,1)S(1)} %collective-permute-done.3.refs_3_), channel_id=1, source_target_pairs={{0,2},{2,0},{4,6},{6,4},{8,10},{10,8},{12,14},{14,12},{1,3},{3,1},... | collective-permute-start | bytes 196616 | tf_op jit(solution)/shard_map/ppermute | solution.py:210
  14.1 0.0 collective-permute-done.2.refs_2_
  14.1 0.0 collective-permute-done.1.refs_1_
  14.1 1.4 %shard_map.65 = (f32[8,24]{1,0:T(8,128)S(1)}, s32[3]{0:T(128)S(4)}, s32[48]{0:T(128)S(4)}, s32[36]{0:T(128)S(4)}, s32[36]{0:T(128)S(4)}, /*index=5*/s32[8,128]{1...) custom-call(s32[8,128]{1,0:T(8,128)S(4)} %get-tuple-element.19.refs_0_, ...), custom_call_target="tpu_custom_call" | custom-call | flops 1000000000 | bytes 9000000 | tf_op jit(solution)/shard_map/pallas_call | solution.py:265
  15.5 0.0 collective-permute-done.7.refs_6_
  15.5 0.8 %shard_map.67.refs_12_ = f32[4,24]{1,0:T(4,128)S(1)} custom-call(s32[8,128]{1,0:T(8,128)S(4)} %get-tuple-element.19.refs_0_, s32[3]{0:T(128)S(4)} %get-tuple-element.25.refs_1_, s32[36]{0:T(128)S(4)} %get-tuple-element.31.refs_2_, s32[8,128]{1,0:T(8,128)S(4)} %get-tuple-element.27.refs_3_, s32[3]{0:T(128)S(4)} %get-tuple-element.28.refs_4_, ...), custom_call_target="tpu_custom_call" | custom-call | flops 1000000000 | bytes 9000000 | tf_op jit(solution)/shard_map/pallas_call | solution.py:265
  16.3 1.1 %collective-permute-done.5.refs_6_ = bf16[8,32,128]{2,1,0:T(8,128)(2,1)S(1)} collective-permute-done((bf16[8,32,128]{2,1,0:T(8,128)(2,1)S(1)}, bf16[8,32,128]{2,1,0:T(8,128)(2,1)S(1)}, u32[]{:S(2)}, u32[]{:S(2)}) %collective-permute-start.5) | collective-permute-done | bytes 65568 | tf_op jit(solution)/shard_map/ppermute | solution.py:210
  17.5 0.0 collective-permute-done.6.refs_7_
  17.5 0.8 %shard_map.68 = f32[16,24]{1,0:T(8,128)S(1)} custom-call(s32[8,128]{1,0:T(8,128)S(4)} %get-tuple-element.19.refs_0_, s32[3]{0:T(128)S(4)} %get-tuple-element.25.refs_1_, s32[36]{0:T(128)S(4)} %get-tuple-element.26.refs_2_, s32[8,128]{1,0:T(8,128)S(4)} %get-tuple-element.27.refs_3_, s32[3]{0:T(128)S(4)} %get-tuple-element.28.refs_4_, ...), custom_call_target="tpu_custom_call" | custom-call | flops 1000000000 | bytes 9000000 | tf_op jit(solution)/shard_map/pallas_call | solution.py:265
  18.3 8.2 %all_to_all.11 = f32[8,2,24]{2,1,0:T(2,128)S(1)} all-to-all(f32[8,2,24]{2,1,0:T(2,128)S(1)} %bitcast.5), channel_id=1, replica_groups={{14,12,10,8,6,4,2,0},{15,13,11,9,7,5,3,1},{30,28,26,24,22,20,18,16},{31..., dimensions={0} | all-to-all | bytes 3072 | tf_op jit(solution)/shard_map/all_to_all | solution.py:286
  26.5 0.6 %shard_map.69 = f32[1,16,24]{2,1,0:T(8,128)} custom-call(f32[16,24]{1,0:T(8,128)S(1)} %bitcast.6), custom_call_target="tpu_custom_call" | custom-call | tf_op jit(solution)/shard_map/pallas_call | solution.py:287
  (1 shorter events, 0.0 us)
Async XLA Ops:
  0.0 10.1 %collective-permute-start = (bf16[128,128,128]{2,1,0:T(8,128)(2,1)}, bf16[128,128,128]{2,1,0:T(8,128)(2,1)S(1)}, u32[]{:S(2)}, u32[]{:S(2)}) collective-permute-start(bf16[128,128,128]{2,1,0:T(8,128)(2,1)} %refs_5_.1), channel_id=1, source_target_pairs={{0,1},{1,0},{2,3},{3,2},{4,5},{5,4},{6,7},{7,6},{8,9},{9,8},{10,11... | collective-permute-start | bytes 12582920 | tf_op jit(solution)/shard_map/ppermute | solution.py:215
  0.5 9.3 %collective-permute-start.4 = (bf16[8,32,128]{2,1,0:T(8,128)(2,1)}, bf16[8,32,128]{2,1,0:T(8,128)(2,1)S(1)}, u32[]{:S(2)}, u32[]{:S(2)}) collective-permute-start(bf16[8,32,128]{2,1,0:T(8,128)(2,1)} %refs_4_.1), channel_id=1, source_target_pairs={{0,2},{2,0},{4,6},{6,4},{8,10},{10,8},{12,14},{14,12},{1,3},{3,1},... | collective-permute-start | bytes 196616 | tf_op jit(solution)/shard_map/ppermute | solution.py:210
  3.0 10.1 %collective-permute-start.3 = (bf16[8,32,128]{2,1,0:T(8,128)(2,1)}, bf16[8,32,128]{2,1,0:T(8,128)(2,1)S(1)}, u32[]{:S(2)}, u32[]{:S(2)}) collective-permute-start(bf16[8,32,128]{2,1,0:T(8,128)(2,1)} %refs_4_.1), channel_id=1, source_target_pairs={{0,8},{2,10},{4,12},{6,14},{8,0},{10,2},{12,4},{14,6},{1,9},{3,11}... | collective-permute-start | bytes 196616 | tf_op jit(solution)/shard_map/ppermute | solution.py:210
  5.6 8.5 %collective-permute-start.2 = (bf16[8,32,128]{2,1,0:T(8,128)(2,1)}, bf16[8,32,128]{2,1,0:T(8,128)(2,1)S(1)}, u32[]{:S(2)}, u32[]{:S(2)}) collective-permute-start(bf16[8,32,128]{2,1,0:T(8,128)(2,1)} %refs_4_.1), channel_id=1, source_target_pairs={{0,12},{2,14},{4,8},{6,10},{8,4},{10,6},{12,0},{14,2},{1,13},{3,15... | collective-permute-start | bytes 196616 | tf_op jit(solution)/shard_map/ppermute | solution.py:210
  9.8 5.7 %collective-permute-start.7 = (bf16[2,8,32,128]{3,2,1,0:T(8,128)(2,1)S(1)}, bf16[2,8,32,128]{3,2,1,0:T(8,128)(2,1)S(1)}, u32[]{:S(2)}, u32[]{:S(2)}) collective-permute-start(bf16[2,8,32,128]{3,2,1,0:T(8,128)(2,1)S(1)} %shard_map.66), channel_id=1, source_target_pairs={{0,4},{2,6},{4,0},{6,2},{8,12},{10,14},{12,8},{14,10},{1,5},{3,7},... | collective-permute-start | bytes 393224 | tf_op jit(solution)/shard_map/ppermute | solution.py:210
  10.1 4.0 %collective-permute-start.1 = (s32[8,128]{1,0:T(8,128)S(1)}, s32[8,128]{1,0:T(8,128)S(1)}, u32[]{:S(2)}, u32[]{:S(2)}) collective-permute-start(s32[8,128]{1,0:T(8,128)S(1)} %get-tuple-element.21), channel_id=1, source_target_pairs={{0,1},{1,0},{2,3},{3,2},{4,5},{5,4},{6,7},{7,6},{8,9},{9,8},{10,11... | collective-permute-start | bytes 12296 | tf_op jit(solution)/shard_map/ppermute | solution.py:255
  10.1 7.4 %collective-permute-start.5 = (bf16[8,32,128]{2,1,0:T(8,128)(2,1)S(1)}, bf16[8,32,128]{2,1,0:T(8,128)(2,1)S(1)}, u32[]{:S(2)}, u32[]{:S(2)}) collective-permute-start(bf16[8,32,128]{2,1,0:T(8,128)(2,1)S(1)} %collective-permute-done.4.refs_4_.other_ref), channel_id=1, source_target_pairs={{0,12},{2,14},{4,8},{6,10},{8,4},{10,6},{12,0},{14,2},{1,13},{3,15... | collective-permute-start | bytes 196616 | tf_op jit(solution)/shard_map/ppermute | solution.py:210
  13.1 4.4 %collective-permute-start.6 = (bf16[8,32,128]{2,1,0:T(8,128)(2,1)S(1)}, bf16[8,32,128]{2,1,0:T(8,128)(2,1)S(1)}, u32[]{:S(2)}, u32[]{:S(2)}) collective-permute-start(bf16[8,32,128]{2,1,0:T(8,128)(2,1)S(1)} %collective-permute-done.3.refs_3_), channel_id=1, source_target_pairs={{0,2},{2,0},{4,6},{6,4},{8,10},{10,8},{12,14},{14,12},{1,3},{3,1},... | collective-permute-start | bytes 196616 | tf_op jit(solution)/shard_map/ppermute | solution.py:210
